TPU v7x, 256 devices: a whole 4x4x8 slice. The times are simulated.
256 devices in a mesh: lat: 8 (over x_hi, y), lon: 32 (over x_lo, z, core).
Axes of the slice: x: 4 (x_hi: 2, x_lo: 2; x = x_hi * 2 + x_lo), y: 4, z: 8, core: 2. Of those that a mesh axis runs over, the one named last changes fastest.
Arguments:
- inputs: bfloat16 [720, 1440, 256], P('lat', 'lon'), may hold values from -6 to 6
- kernel: bfloat16 [3, 3, 256, 256], replicated, may hold values from -0.125 to 0.125
- cotangent: bfloat16 [720, 1440, 256], P('lat', 'lon'), may hold values from -6 to 6
Outputs:
- outputs: bfloat16 [720, 1440, 256], P('lat', 'lon')
- input_grad: bfloat16 [720, 1440, 256], P('lat', 'lon')
- kernel_grad: float32 [3, 3, 256, 256], replicated
All inputs are finite; a program needn't handle non-finite values.
Results may differ from a plain program's by a relative error of at most 0.001.
Values may be sent and summed in bfloat16 or wider, within the bound.
A program may use at most 192 MiB of HBM per device.

v0:
```python
import math

import jax
import jax.numpy as jnp
from jax import lax
from jax.sharding import PartitionSpec as P


def with_halo(cells, sides, width):
    for axis, dim in sides:
        count = lax.axis_size(axis)
        head = lax.slice_in_dim(cells, 0, width, axis=dim)
        tail = lax.slice_in_dim(cells, cells.shape[dim] - width, cells.shape[dim], axis=dim)
        cells = jnp.concatenate(
            [
                lax.ppermute(tail, axis, [(i, (i + 1) % count) for i in range(count)]),
                cells,
                lax.ppermute(head, axis, [((i + 1) % count, i) for i in range(count)]),
            ],
            axis=dim,
        )
    return cells


def from_behind(value, axis, steps):
    count = lax.axis_size(axis)
    pairs = [(source, (source + steps) % count) for source in range(count)]
    return lax.ppermute(value, axis, pairs)


def patches(padded, rows, cols):
    pieces = [
        padded[row_tap : row_tap + rows, col_tap : col_tap + cols]
        for row_tap in range(3)
        for col_tap in range(3)
    ]
    return jnp.concatenate(pieces, axis=-1).reshape(rows * cols, -1)


def surround(field):
    return with_halo(field, (("lat", 0), ("lon", 1)), 1)


def polar(padded):
    both = jnp.stack([padded[1], padded[-2]])
    moved = from_behind(both, "lon", lax.axis_size("lon") // 2)
    return (moved[0], moved[1])


def edge_term(row_data, weights, cols, width):
    stacked = jnp.concatenate([row_data[offset : offset + cols] for offset in range(3)], axis=-1)
    return jnp.dot(stacked, weights.reshape(-1, width), preferred_element_type=jnp.float32)


def local(inputs, kernel, cotangent):
    rows, cols, width = inputs.shape
    north = lax.axis_index("lat") == 0
    south = lax.axis_index("lat") == lax.axis_size("lat") - 1
    padded = surround(inputs)
    top, bottom = polar(padded)
    padded = jnp.concatenate(
        [
            jnp.where(north, top, padded[0])[None],
            padded[1:-1],
            jnp.where(south, bottom, padded[-1])[None],
        ],
        0,
    )
    columns = patches(padded, rows, cols)
    outputs = jnp.dot(columns, kernel.reshape(-1, width), preferred_element_type=jnp.float32)
    outputs = outputs.reshape(rows, cols, width).astype(jnp.bfloat16)
    flat_grad = cotangent.reshape(-1, width)
    local_grad = lax.dot_general(
        columns, flat_grad, (((0,), (0,)), ((), ())), preferred_element_type=jnp.float32
    )
    local_grad = local_grad.reshape(3, 3, width, width)
    padded_grad = surround(cotangent)
    grad_top, grad_bottom = polar(padded_grad)
    empty_row = jnp.zeros_like(padded_grad[0])
    padded_grad = jnp.concatenate(
        [
            jnp.where(north, empty_row, padded_grad[0])[None],
            padded_grad[1:-1],
            jnp.where(south, empty_row, padded_grad[-1])[None],
        ],
        0,
    )
    flipped = jnp.transpose(kernel[::-1, ::-1], (0, 1, 3, 2))
    input_grad = jnp.dot(
        patches(padded_grad, rows, cols),
        flipped.reshape(-1, width),
        preferred_element_type=jnp.float32,
    )
    input_grad = input_grad.reshape(rows, cols, width)
    north_term = edge_term(grad_top, flipped[2], cols, width)
    south_term = edge_term(grad_bottom, flipped[0], cols, width)
    input_grad = input_grad.at[0].add(jnp.where(north, north_term, 0.0))
    input_grad = input_grad.at[-1].add(jnp.where(south, south_term, 0.0))
    factor = 1.0 / math.sqrt(rows * cols * lax.axis_size("lat") * lax.axis_size("lon"))
    summed = lax.psum(local_grad, ("lat", "lon"))
    return (outputs, input_grad.astype(jnp.bfloat16), summed * factor)


def solution(mesh):
    in_specs = (P("lat", "lon", None), P(), P("lat", "lon", None))
    out_specs = (P("lat", "lon", None), P("lat", "lon", None), P())
    return jax.shard_map(local, mesh=mesh, in_specs=in_specs, out_specs=out_specs, check_vma=False)
```

profile of v0, /device:TPU:1, one launch (start us, length us, event | category | flops | bytes accessed | tf_op | source)
XLA Modules:
  0.0 426.6 jit_solution(5525735376347575952)
XLA Ops:
  7.2 0.8 fusion.70
  8.0 6.0 %collective-permute-start.1 = (bf16[1,45,256]{2,1,0:T(8,128)(2,1)S(1)}, bf16[1,45,256]{2,1,0:T(8,128)(2,1)S(1)}, u32[]{:S(2)}, u32[]{:S(2)}) collective-permute-start(bf16[1,45,256]{2,1,0:T(8,128)(2,1)S(1)} %get-tuple-element.37), channel_id=1, source_target_pairs={{32,0},{64,32},{96,64},{128,96},{160,128},{192,160},{224,192},{0,2... | collective-permute-start | bytes 69128 | tf_op jit(solution)/shard_map/ppermute | solution.py:18
  14.0 1.4 fusion.69
  15.4 5.1 %collective-permute-start.6 = (bf16[1,45,256]{2,1,0:T(8,128)(2,1)}, bf16[1,45,256]{2,1,0:T(8,128)(2,1)S(1)}, u32[]{:S(2)}, u32[]{:S(2)}) collective-permute-start(bf16[1,45,256]{2,1,0:T(8,128)(2,1)} %get-tuple-element.35), channel_id=1, source_target_pairs={{32,0},{64,32},{96,64},{128,96},{160,128},{192,160},{224,192},{0,2... | collective-permute-start | bytes 69128 | tf_op jit(solution)/shard_map/ppermute | solution.py:18
  20.5 1.6 copy.6
  22.1 0.9 fusion.71
  23.1 1.1 rev.3
  24.2 1.9 reshape.103
  26.1 0.9 collective-permute-done.5
  27.3 4.3 collective-permute-start.7
  31.9 1.8 collective-permute-start.2
  33.7 0.7 collective-permute-start.3
  34.4 1.3 collective-permute-done.8
  35.8 0.5 collective-permute-start.9
  36.3 1.4 collective-permute-done.3
  37.7 0.6 collective-permute-start.4
  38.3 1.6 pad_maximum_fusion.1
  40.1 1.6 fusion.7
  41.7 2.9 fusion.5
  44.6 2.9 fusion.19
  47.5 2.8 fusion.18
  50.3 1.6 constant_dynamic-update-slice_fusion.7
  51.9 3.1 fusion.17
  54.9 1.7 fusion.3
  56.6 2.9 fusion.1
  59.5 2.9 fusion.16
  62.4 9.9 %fusion.72 = f32[90,45,256]{2,1,0:T(8,128)S(1)} fusion(bf16[90,45,2304]{2,1,0:T(8,128)(2,1)} %fusion.16, bf16[2304,256,1]{1,0,2:T(8,128)(2,1)S(1)} %bitcast.50), kind=kOutput, calls=%fused_computation.114 | convolution fusion | flops 4777574400 | bytes 23989248 | tf_op jit(solution)/shard_map/dot_general | solution.py:89
  72.2 1.6 pad_maximum_fusion
  74.0 0.8 copy-done.4
  74.8 0.2 fusion.62
  75.0 0.2 fusion.28
  75.2 1.6 convert_element_type.7
  76.9 1.6 fusion.15
  78.5 2.8 fusion.13
  81.4 2.9 fusion.23
  84.3 2.8 fusion.22
  87.0 1.6 constant_dynamic-update-slice_fusion.3
  88.7 3.1 fusion.21
  91.7 1.7 fusion.11
  93.4 2.8 fusion.9
  96.2 2.8 fusion.20
  99.1 19.4 %reshape.99 = bf16[4050,2304]{1,0:T(8,128)(2,1)} reshape(bf16[90,45,2304]{2,1,0:T(8,128)(2,1)} %fusion.20) | data formatting | bytes 37324800 | tf_op jit(solution)/shard_map/reshape | solution.py:37
  118.4 25.0 %copy.7 = bf16[4050,2304]{0,1:T(8,128)(2,1)} copy(bf16[4050,2304]{1,0:T(8,128)(2,1)} %reshape.99) | data formatting | bytes 37324800 | tf_op jit(solution)/shard_map/reshape | solution.py:37
  143.4 10.6 %fusion.24 = f32[3,3,256,256]{3,2,1,0:T(8,128)} fusion(bf16[3,3,256,4050]{3,2,1,0:T(8,128)(2,1)} %bitcast.46, bf16[4050,256,1,1]{1,0,2,3:T(8,128)(2,1)S(1)} %copy-done.2), kind=kOutput, calls=%fused_computation.42 | convolution fusion | flops 4777574400 | bytes 23095296 | tf_op jit(solution)/shard_map/dot_general | solution.py:73
  154.0 1.2 copy-done.5
  155.3 11.5 %convolution_convert_fusion = bf16[90,45,256]{2,1,0:T(8,128)(2,1)} fusion(bf16[90,45,2304]{2,1,0:T(8,128)(2,1)} %fusion.20, bf16[2304,256,1]{1,0,2:T(8,128)(2,1)S(1)} %bitcast.49), kind=kOutput, calls=%fused_computation.44 | convolution fusion | flops 4778611200 | bytes 21915648 | tf_op jit(solution)/shard_map/dot_general | solution.py:70
  166.8 249.3 %all-reduce.2.cloned.1.call-done = f32[3,3,256,256]{3,2,1,0:T(8,128)} async-done(((f32[3,3,256,256]{3,2,1,0:T(8,128)}), f32[3,3,256,256]{3,2,1,0:T(8,128)}) %all-reduce.2.cloned.1.call-update) | async-done | bytes 2359312 | tf_op jit(solution)/shard_map/psum | solution.py:100
  416.1 3.3 broadcast_multiply_fusion
  (40 shorter events, 1.2 us)
Async XLA Ops:
  7.2 408.9 %all-reduce.2.cloned.1.call-start = ((), (), s32[]{:S(2)}) async-start(), calls=%async_computation | async-start | bytes 4718592 | tf_op jit(solution)/shard_map/psum | solution.py:100
  8.0 23.8 %collective-permute-start.1 = (bf16[1,45,256]{2,1,0:T(8,128)(2,1)S(1)}, bf16[1,45,256]{2,1,0:T(8,128)(2,1)S(1)}, u32[]{:S(2)}, u32[]{:S(2)}) collective-permute-start(bf16[1,45,256]{2,1,0:T(8,128)(2,1)S(1)} %get-tuple-element.37), channel_id=1, source_target_pairs={{32,0},{64,32},{96,64},{128,96},{160,128},{192,160},{224,192},{0,2... | collective-permute-start | bytes 69128 | tf_op jit(solution)/shard_map/ppermute | solution.py:18
  14.0 17.6 %collective-permute-start = (bf16[1,45,256]{2,1,0:T(8,128)(2,1)S(1)}, bf16[1,45,256]{2,1,0:T(8,128)(2,1)S(1)}, u32[]{:S(2)}, u32[]{:S(2)}) collective-permute-start(bf16[1,45,256]{2,1,0:T(8,128)(2,1)S(1)} %get-tuple-element.38), channel_id=1, source_target_pairs={{0,32},{32,64},{64,96},{96,128},{128,160},{160,192},{192,224},{224... | collective-permute-start | bytes 69128 | tf_op jit(solution)/shard_map/ppermute | solution.py:16
  15.4 11.7 %collective-permute-start.6 = (bf16[1,45,256]{2,1,0:T(8,128)(2,1)}, bf16[1,45,256]{2,1,0:T(8,128)(2,1)S(1)}, u32[]{:S(2)}, u32[]{:S(2)}) collective-permute-start(bf16[1,45,256]{2,1,0:T(8,128)(2,1)} %get-tuple-element.35), channel_id=1, source_target_pairs={{32,0},{64,32},{96,64},{128,96},{160,128},{192,160},{224,192},{0,2... | collective-permute-start | bytes 69128 | tf_op jit(solution)/shard_map/ppermute | solution.py:18
  20.5 6.5 %collective-permute-start.5 = (bf16[1,45,256]{2,1,0:T(8,128)(2,1)}, bf16[1,45,256]{2,1,0:T(8,128)(2,1)S(1)}, u32[]{:S(2)}, u32[]{:S(2)}) collective-permute-start(bf16[1,45,256]{2,1,0:T(8,128)(2,1)} %get-tuple-element.36), channel_id=1, source_target_pairs={{0,32},{32,64},{64,96},{96,128},{128,160},{160,192},{192,224},{224... | collective-permute-start | bytes 69128 | tf_op jit(solution)/shard_map/ppermute | solution.py:16
  22.1 2.0 copy-start
  27.0 4.6 %copy-start.1 = (bf16[90,45,256]{2,1,0:T(8,128)(2,1)S(1)}, bf16[90,45,256]{2,1,0:T(8,128)(2,1)}, u32[]{:S(2)}) copy-start(bf16[90,45,256]{2,1,0:T(8,128)(2,1)} %param.7) | copy-start | bytes 6220804
  27.3 7.1 %collective-permute-start.7 = (bf16[92,1,256]{2,1,0:T(2,128)(2,1)S(1)}, bf16[92,1,256]{2,1,0:T(2,128)(2,1)S(1)}, u32[]{:S(2)}, u32[]{:S(2)}) collective-permute-start(bf16[92,1,256]{2,1,0:T(2,128)(2,1)S(1)} %get-tuple-element.31), channel_id=1, source_target_pairs={{0,1},{1,2},{2,3},{3,4},{4,5},{5,6},{6,7},{7,8},{8,9},{9,10},{10,1... | collective-permute-start | bytes 141320 | tf_op jit(solution)/shard_map/ppermute | solution.py:16
  31.6 4.2 collective-permute-start.8
  31.9 4.4 %collective-permute-start.2 = (bf16[92,1,256]{2,1,0:T(2,128)(2,1)S(1)}, bf16[92,1,256]{2,1,0:T(2,128)(2,1)S(1)}, u32[]{:S(2)}, u32[]{:S(2)}) collective-permute-start(bf16[92,1,256]{2,1,0:T(2,128)(2,1)S(1)} %get-tuple-element.33), channel_id=1, source_target_pairs={{0,1},{1,2},{2,3},{3,4},{4,5},{5,6},{6,7},{7,8},{8,9},{9,10},{10,1... | collective-permute-start | bytes 141320 | tf_op jit(solution)/shard_map/ppermute | solution.py:16
  33.7 4.0 collective-permute-start.3
  35.8 38.2 %collective-permute-start.9 = (bf16[2,47,256]{2,1,0:T(8,128)(2,1)S(1)}, bf16[2,47,256]{2,1,0:T(8,128)(2,1)S(1)}, u32[]{:S(2)}, u32[]{:S(2)}) collective-permute-start(bf16[2,47,256]{2,1,0:T(8,128)(2,1)S(1)} %fusion.57), channel_id=1, source_target_pairs={{0,16},{1,17},{2,18},{3,19},{4,20},{5,21},{6,22},{7,23},{8,24},{9,... | collective-permute-start | bytes 144392 | tf_op jit(solution)/shard_map/ppermute | solution.py:28
  37.7 39.1 %collective-permute-start.4 = (bf16[2,47,256]{2,1,0:T(8,128)(2,1)S(1)}, bf16[2,47,256]{2,1,0:T(8,128)(2,1)S(1)}, u32[]{:S(2)}, u32[]{:S(2)}) collective-permute-start(bf16[2,47,256]{2,1,0:T(8,128)(2,1)S(1)} %fusion.54), channel_id=1, source_target_pairs={{0,16},{1,17},{2,18},{3,19},{4,20},{5,21},{6,22},{7,23},{8,24},{9,... | collective-permute-start | bytes 144392 | tf_op jit(solution)/shard_map/ppermute | solution.py:28
  59.5 2.9 copy-start.6
  73.8 1.0 copy-start.4
  73.8 1.2 copy-start.3
  118.4 25.0 %copy-start.2 = (bf16[4050,256,1,1]{1,0,2,3:T(8,128)(2,1)S(1)}, bf16[4050,256,1,1]{1,0,2,3:T(8,128)(2,1)}, u32[]{:S(2)}) copy-start(bf16[4050,256,1,1]{1,0,2,3:T(8,128)(2,1)} %reshape.103) | copy-start | bytes 6220804
  154.0 1.3 copy-start.5
Sparse Core Ops, SparseCore 0:
  154.2 261.8 all-reduce.1
where the time goes:
time: 435 us; the launch traced here: 427 us
  waiting for transfers between devices  253 us (58%)
  local copies, waits for them, and re-layouts  58.2 us (13%)
  other arithmetic  49.3 us (11%)
  matrix products  32.4 us (7%)
  starting transfers between devices  19 us (4%)
  between operations  14.7 us (3%)
    psum x1, waiting for transfers between devices, local(): summed = lax.psum(local_grad, ('lat', 'lon'))  249 us
    reshape x2, local copies, waits for them, and re-layouts, patches(): return jnp.concatenate(pieces, axis=-1).reshape(rows * cols, -1)  44.3 us
    unnamed x14, other arithmetic  35.5 us
    ppermute x4, starting transfers between devices, with_halo(): lax.ppermute(head, axis, [((i + 1) % count, i) for i in range(count)])  11.8 us
    dot_general x1, matrix products, local(): jnp.dot(columns, kernel.reshape(-1, width), preferred_element_type=jnp.fl...  11.5 us
    dot_general x1, matrix products, local(): lax.dot_general(columns, flat_grad, (((0,), (0,)), ((), ())), preferred_e...  10.6 us
    dot_general x1, matrix products, local(): jnp.dot(patches(padded_grad, rows, cols), flipped.reshape(-1, width), pre...  9.89 us
  transfers between devices with their start and end apart: 11, of which 4 were waited for; matrix products, arithmetic and copies ran while one was open for 13% of the time, Pallas kernels for 0%

commit v1 on v0

v1 whole, which is shorter than its diff:
```python
import functools
import math

import jax
import jax.numpy as jnp
from jax import lax
from jax.experimental import pallas as pl
from jax.experimental.pallas import tpu as pltpu
from jax.sharding import PartitionSpec as P

MESH = pl.DeviceIdType.MESH
F32 = jnp.float32
BF16 = jnp.bfloat16

ROWS, COLS, CH = 90, 45, 256
PITCH = 48
FLAT = (ROWS + 2) * PITCH + 32
DEPTH = 4352
NX, NY, NZ = 4, 4, 8
TILE = 15
TILES = ROWS // TILE
TAPS = 9
GAP = 2
STEPS = TAPS + 2 * TILES


def rows_at(row, count):
    return pl.ds(pl.multiple_of(row * PITCH, 16), count)


def kernel(
    scale,
    x_hbm, w_hbm, c_hbm,
    out_hbm, grad_hbm, kg_hbm,
    x_in, c_in, w,
    xs, cs, xt, x_rows, c_rows, c_halo,
    col_send, col_recv,
    out_v, grad_v,
    term, pair_recv, half, recv1, sum1, recv2, recv3, final,
    load_sem, store_sem, kg_sem,
    row_send_sem, row_recv_sem, col_send_sem, col_recv_sem,
    ar_send_sem, ar_recv_sem,
):
    lat, lon = lax.axis_index("lat"), lax.axis_index("lon")
    x_hi, y = lat // 4, lat % 4
    x_lo, z, core = lon // 16, (lon // 2) % 8, lon % 2
    xc = x_hi * 2 + x_lo

    def device(xx, yy, zz, cc):
        return ((xx // 2) * 4 + yy, ((xx % 2) * 8 + zz) * 2 + cc)

    north, south = lat == 0, lat == 7
    across = (lon + 16) % 32
    up = (jnp.where(north, 0, lat - 1), jnp.where(north, across, lon))
    down = (jnp.where(south, 7, lat + 1), jnp.where(south, across, lon))
    left, right = (lat, (lon + 31) % 32), (lat, (lon + 1) % 32)
    other = device(xc, y, z, 1 - core)

    loads = [
        pltpu.make_async_copy(c_hbm, c_in, load_sem.at[0]),
        pltpu.make_async_copy(x_hbm, x_in, load_sem.at[1]),
        pltpu.make_async_copy(w_hbm, w, load_sem.at[2]),
    ]
    for load in loads:
        load.start()

    barrier = pltpu.get_barrier_semaphore()
    friends = [up, down, left, right, other]
    friends += [device((xc + d) % NX, y, z, core) for d in range(1, NX)]
    friends += [device(xc, (y + d) % NY, z, core) for d in range(1, NY)]
    friends += [device(xc, y, (z + d) % NZ, core) for d in range(1, NZ)]
    for friend in friends:
        pl.semaphore_signal(barrier, inc=1, device_id=friend, device_id_type=MESH)
    pl.semaphore_wait(barrier, len(friends))

    def row_copies(which, source, target):
        to_up, to_down = jnp.where(north, 0, 1), jnp.where(south, 1, 0)
        return [
            pltpu.make_async_remote_copy(
                src_ref=source.at[0], dst_ref=target.at[to_up],
                send_sem=row_send_sem.at[which, 0], recv_sem=row_recv_sem.at[which, to_up],
                device_id=up, device_id_type=MESH,
            ),
            pltpu.make_async_remote_copy(
                src_ref=source.at[ROWS - 1], dst_ref=target.at[to_down],
                send_sem=row_send_sem.at[which, 1], recv_sem=row_recv_sem.at[which, to_down],
                device_id=down, device_id_type=MESH,
            ),
        ]

    def row_wait(which, target):
        for side in range(2):
            pltpu.make_async_copy(target.at[side], target.at[side], row_recv_sem.at[which, side]).wait()

    def col_copies(which):
        return [
            pltpu.make_async_remote_copy(
                src_ref=col_send.at[which, side], dst_ref=col_recv.at[which, side],
                send_sem=col_send_sem.at[which, side], recv_sem=col_recv_sem.at[which, side],
                device_id=to, device_id_type=MESH,
            )
            for side, to in ((0, right), (1, left))
        ]

    def pack_columns(which, block, rows):
        for side, col in ((0, COLS - 1), (1, 0)):
            col_send[which, side, 1 : ROWS + 1] = block[:, col : col + 1, :].astype(F32)
            col_send[which, side, 0:1] = rows[0:1, col : col + 1, :].astype(F32)
            col_send[which, side, ROWS + 1 :] = rows[1:2, col : col + 1, :].astype(F32)

    sends = []
    for which, source, target in ((0, c_hbm, c_rows), (1, x_hbm, x_rows)):
        for copy in row_copies(which, source, target):
            copy.start()
            sends.append(copy)

    def shifted(row):
        wide = row.astype(F32)
        one = jnp.zeros((1, CH), F32)
        return (
            jnp.concatenate([one, wide, one, one], 0).astype(BF16),
            jnp.concatenate([wide, one, one, one], 0).astype(BF16),
            jnp.concatenate([wide[1:], one, one, one, one], 0).astype(BF16),
        )

    def spread(block, target):
        @pl.loop(0, ROWS)
        def _(r):
            for b, value in enumerate(shifted(block[r])):
                target[b, rows_at(r + 1, PITCH), :] = value

        for b in range(3):
            target[b, 0:PITCH, :] = jnp.zeros((PITCH, CH), BF16)
            target[b, (ROWS + 1) * PITCH :, :] = jnp.zeros((FLAT - (ROWS + 1) * PITCH, CH), BF16)

    loads[0].wait()
    spread(c_in, cs)
    loads[1].wait()
    spread(x_in, xs)
    for i in range(DEPTH // 256):
        xt[:, i * 256 : (i + 1) * 256] = xs[1, PITCH + i * 256 : PITCH + (i + 1) * 256, :].T

    row_wait(0, c_rows)
    row_wait(1, x_rows)
    pack_columns(0, c_in, c_rows)
    for copy in col_copies(0):
        copy.start()
        sends.append(copy)
    pack_columns(1, x_in, x_rows)
    for copy in col_copies(1):
        copy.start()
        sends.append(copy)
    loads[2].wait()

    for side in range(2):
        for b, value in enumerate(shifted(c_rows[side])):
            c_halo[b, side] = value
        for b, value in enumerate(shifted(x_rows[side])):
            xs[b, side * (ROWS + 1) * PITCH : side * (ROWS + 1) * PITCH + PITCH, :] = value

    def fill_columns(which, target):
        for side, b, cell in ((0, 0, 0), (1, 2, COLS - 1)):
            @pl.loop(1, ROWS + 1)
            def _(r):
                base = pl.multiple_of(r * PITCH + (cell // 16) * 16, 16)
                block = target[b, pl.ds(base, 16), :].astype(F32)
                at = lax.broadcasted_iota(jnp.int32, (16, CH), 0) == cell % 16
                target[b, pl.ds(base, 16), :] = jnp.where(at, col_recv[which, side, r], block).astype(BF16)

    def fill_row(which, row, side, b, cell):
        at = lax.broadcasted_iota(jnp.int32, (PITCH, CH), 0) == cell
        edge = col_recv[which, side, row]
        return lambda value: jnp.where(at, edge, value.astype(F32)).astype(BF16)

    def tap_of(t):
        return (1 + 2 * (t % 3)) % 3, (1 + 2 * (t // 3)) % 3

    top_tap = jnp.where(north, 0, 2)
    bottom_tap = jnp.where(south, 2, 0)

    def pair_copy(t):
        return pltpu.make_async_remote_copy(
            src_ref=term.at[t, 1 - core], dst_ref=pair_recv.at[t],
            send_sem=ar_send_sem.at[0, t], recv_sem=ar_recv_sem.at[0, t],
            device_id=other, device_id_type=MESH,
        )

    def axes(t):
        odd = t % 2
        first = odd * y + (1 - odd) * xc
        second = odd * xc + (1 - odd) * y
        return odd, first, second

    def first_peer(t, d):
        odd = t % 2
        return device((xc + d * (1 - odd)) % NX, (y + d * odd) % NY, z, core)

    def second_peer(t, d):
        odd = t % 2
        return device((xc + d * odd) % NX, (y + d * (1 - odd)) % NY, z, core)

    def remote(src, dst, phase, t, to):
        pltpu.make_async_remote_copy(
            src_ref=src, dst_ref=dst, send_sem=ar_send_sem.at[phase, t], recv_sem=ar_recv_sem.at[phase, t],
            device_id=to, device_id_type=MESH,
        ).start()

    def arrived(ref, phase, t):
        pltpu.make_async_copy(ref, ref, ar_recv_sem.at[phase, t]).wait()

    def phase1(t):
        arrived(pair_recv.at[t], 0, t)
        half[t] = term[t, core] + pair_recv[t]
        _, first, _ = axes(t)
        for d in range(1, 4):
            remote(half.at[t, (first + d) % 4], recv1.at[t, d - 1], 1, t, first_peer(t, d))

    def phase2(t):
        arrived(recv1.at[t], 1, t)
        _, first, second = axes(t)
        sum1[t] = (half[t, first] + recv1[t, 0]) + (recv1[t, 1] + recv1[t, 2])
        for d in range(1, 4):
            remote(sum1.at[t, (second + d) % 4], recv2.at[t, d - 1], 2, t, second_peer(t, d))

    def phase3(t):
        arrived(recv2.at[t], 2, t)
        _, _, second = axes(t)
        recv3[t, z] = (sum1[t, second] + recv2[t, 0]) + (recv2[t, 1] + recv2[t, 2])
        for d in range(1, 8):
            remote(recv3.at[t, z], recv3.at[t, z], 3, t, device(xc, y, (z + d) % NZ, core))

    def phase4(t):
        arrived(recv3.at[t, 0:7], 3, t)
        _, first, second = axes(t)
        pairs = [recv3[t, 2 * i] + recv3[t, 2 * i + 1] for i in range(4)]
        final[t, core, first, second] = ((pairs[0] + pairs[1]) + (pairs[2] + pairs[3])) * scale
        piece = final.at[t, core, first, second]
        for d in range(1, 4):
            remote(piece, piece, 4, t, second_peer(t, d))

    def phase5(t):
        arrived(recv2.at[t], 4, t)
        _, first, _ = axes(t)
        piece = final.at[t, core, first]
        for d in range(1, 4):
            remote(piece, piece, 5, t, first_peer(t, d))

    def phase6(t):
        arrived(recv1.at[t], 5, t)
        remote(final.at[t, core], final.at[t, core], 6, t, other)

    def kg_copy(t, side):
        a, b = tap_of(t)
        return pltpu.make_async_copy(
            final.at[t, side], kg_hbm.at[a * 3 + b, :, :, :, side * 128 : side * 128 + 128], kg_sem.at[t, side]
        )

    def phase7(t):
        arrived(pair_recv.at[t], 6, t)
        for side in range(2):
            kg_copy(t, side).start()

    phases = [phase1, phase2, phase3, phase4, phase5, phase6, phase7]

    def weight_tap(t):
        a, b = tap_of(t)
        res = jnp.dot(xt[...], cs[2 - b, rows_at(2 - a, DEPTH), :], preferred_element_type=F32)
        term[t, 0] = res[:, :128].reshape(4, 4, 16, 128)
        term[t, 1] = res[:, 128:].reshape(4, 4, 16, 128)
        for side, tap, row in ((0, top_tap, 1), (1, bottom_tap, ROWS)):
            @pl.when(a == tap)
            def _():
                more = lax.dot_general(
                    xs[1, row * PITCH : row * PITCH + PITCH, :], c_halo[2 - b, side],
                    (((0,), (0,)), ((), ())), preferred_element_type=F32,
                )
                term[t, 0] += more[:, :128].reshape(4, 4, 16, 128)
                term[t, 1] += more[:, 128:].reshape(4, 4, 16, 128)
        pair_copy(t).start()

    def out_copy(i, which):
        value, target = ((out_v, out_hbm), (grad_v, grad_hbm))[which]
        part = pl.ds(i * TILE, TILE)
        return pltpu.make_async_copy(value.at[part], target.at[part], store_sem.at[which, i])

    def out_tile(i):
        acc = None
        for a in range(3):
            for b in range(3):
                part = jnp.dot(
                    xs[b, rows_at(i * TILE + a, TILE * PITCH), :], w[a, b], preferred_element_type=F32
                )
                acc = part if acc is None else acc + part
        out_v[pl.ds(i * TILE, TILE)] = acc.astype(BF16).reshape(TILE, PITCH, CH)[:, :COLS]
        out_copy(i, 0).start()

    def times_transposed(rows, weights):
        return lax.dot_general(rows, weights, (((1,), (1,)), ((), ())), preferred_element_type=F32)

    def grad_rows(row, count):
        acc = None
        for a in range(3):
            for b in range(3):
                part = times_transposed(cs[2 - b, rows_at(row + 2 - a, count * PITCH), :], w[a, b])
                acc = part if acc is None else acc + part
        return acc

    def grad_tile(i):
        grad_v[pl.ds(i * TILE, TILE)] = (
            grad_rows(i * TILE, TILE).astype(BF16).reshape(TILE, PITCH, CH)[:, :COLS]
        )
        for side, tile, row, tap in ((0, 0, 0, top_tap), (1, TILES - 1, ROWS - 1, bottom_tap)):
            @pl.when(i == tile)
            def _():
                acc = grad_rows(row, 1)
                for b in range(3):
                    acc = acc + times_transposed(c_halo[2 - b, side], w[tap, b])
                grad_v[row] = acc.astype(BF16)[:COLS]
        out_copy(i, 1).start()

    @pl.loop(0, TAPS + GAP * len(phases))
    def _(s):
        for p in range(len(phases), 0, -1):
            t = s - GAP * p

            @pl.when((t >= 0) & (t < TAPS))
            def _():
                phases[p - 1](t)

        @pl.when(s == 3)
        def _():
            for side in range(2):
                pltpu.make_async_copy(
                    col_recv.at[0, side], col_recv.at[0, side], col_recv_sem.at[0, side]
                ).wait()
            fill_columns(0, cs)
            for side, b, cell in ((0, 0, 0), (1, 2, COLS - 1)):
                for end in range(2):
                    put = fill_row(0, end * (ROWS + 1), side, b, cell)
                    c_halo[b, end] = put(c_halo[b, end])

        @pl.when(s < TAPS)
        def _():
            weight_tap(s)

        @pl.when(s == TAPS)
        def _():
            for side in range(2):
                pltpu.make_async_copy(
                    col_recv.at[1, side], col_recv.at[1, side], col_recv_sem.at[1, side]
                ).wait()
            fill_columns(1, xs)
            for side, b, cell in ((0, 0, 0), (1, 2, COLS - 1)):
                for end in range(2):
                    put = fill_row(1, end * (ROWS + 1), side, b, cell)
                    place = slice(end * (ROWS + 1) * PITCH, end * (ROWS + 1) * PITCH + PITCH)
                    xs[b, place, :] = put(xs[b, place, :])

        @pl.when((s >= TAPS) & (s < TAPS + TILES))
        def _():
            out_tile(s - TAPS)

        @pl.when((s >= TAPS + TILES) & (s < STEPS))
        def _():
            grad_tile(s - TAPS - TILES)

    for copy in sends:
        copy.wait_send()

    @pl.loop(0, TAPS)
    def _(t):
        for phase, ref in enumerate((pair_recv, recv1, recv2, recv3.at[:, 0:7], recv2, recv1, pair_recv)):
            pltpu.make_async_copy(ref.at[t], ref.at[t], ar_send_sem.at[phase, t]).wait()
        for side in range(2):
            kg_copy(t, side).wait()

    @pl.loop(0, TILES)
    def _(i):
        for which in range(2):
            out_copy(i, which).wait()


def local(inputs, weights, cotangent):
    scale = 1.0 / math.sqrt(ROWS * COLS * lax.axis_size("lat") * lax.axis_size("lon"))
    block = jax.ShapeDtypeStruct((ROWS, COLS, CH), BF16)
    anywhere = pl.BlockSpec(memory_space=pl.ANY)
    dma = pltpu.SemaphoreType.DMA
    outputs, grad, kg = pl.pallas_call(
        functools.partial(kernel, scale),
        out_shape=(block, block, jax.ShapeDtypeStruct((TAPS, 4, 4, 16, CH), F32)),
        in_specs=[anywhere] * 3,
        out_specs=(anywhere,) * 3,
        scratch_shapes=[
            pltpu.VMEM((ROWS, COLS, CH), BF16),
            pltpu.VMEM((ROWS, COLS, CH), BF16),
            pltpu.VMEM((3, 3, CH, CH), BF16),
            pltpu.VMEM((3, FLAT, CH), BF16),
            pltpu.VMEM((3, FLAT, CH), BF16),
            pltpu.VMEM((CH, DEPTH), BF16),
            pltpu.VMEM((2, COLS, CH), BF16),
            pltpu.VMEM((2, COLS, CH), BF16),
            pltpu.VMEM((3, 2, PITCH, CH), BF16),
            pltpu.VMEM((2, 2, ROWS + 2, 1, CH), F32),
            pltpu.VMEM((2, 2, ROWS + 2, 1, CH), F32),
            pltpu.VMEM((ROWS, COLS, CH), BF16),
            pltpu.VMEM((ROWS, COLS, CH), BF16),
            pltpu.VMEM((TAPS, 2, 4, 4, 16, 128), F32),
            pltpu.VMEM((TAPS, 4, 4, 16, 128), F32),
            pltpu.VMEM((TAPS, 4, 4, 16, 128), F32),
            pltpu.VMEM((TAPS, 3, 4, 16, 128), F32),
            pltpu.VMEM((TAPS, 4, 16, 128), F32),
            pltpu.VMEM((TAPS, 3, 16, 128), F32),
            pltpu.VMEM((TAPS, 8, 16, 128), F32),
            pltpu.VMEM((TAPS, 2, 4, 4, 16, 128), F32),
            dma((3,)),
            dma((2, TILES)),
            dma((TAPS, 2)),
            dma((2, 2)),
            dma((2, 2)),
            dma((2, 2)),
            dma((2, 2)),
            dma((7, TAPS)),
            dma((7, TAPS)),
        ],
        compiler_params=pltpu.CompilerParams(
            collective_id=0, has_side_effects=True, vmem_limit_bytes=56 * 2**20
        ),
        cost_estimate=pl.CostEstimate(flops=15 * 10**9, bytes_accessed=12 * 10**6, transcendentals=0),
    )(inputs, weights, cotangent)
    return outputs, grad, kg.reshape(3, 3, CH, CH)


def solution(mesh):
    in_specs = (P("lat", "lon", None), P(), P("lat", "lon", None))
    out_specs = (P("lat", "lon", None), P("lat", "lon", None), P())
    return jax.shard_map(local, mesh=mesh, in_specs=in_specs, out_specs=out_specs, check_vma=False)
```

time: 435 us -> 70.3 us (0.16); the launches traced: 427 us -> 70.2 us
  waiting for transfers between devices: 253 us -> 0 us
  Pallas kernels: 0 us -> 62.4 us
  local copies, waits for them, and re-layouts: 58.2 us -> 7.15 us
  other arithmetic: 49.3 us -> 0 us
  matrix products: 32.4 us -> 0 us
  starting transfers between devices: 19 us -> 0 us
  between operations: 14.7 us -> 0.65 us
    psum x1 -> x0, waiting for transfers between devices: 249 us -> none  [local(): summed = lax.psum(local_grad, ('lat', 'lon'))]
    pallas_call x0 -> x1, Pallas kernels: none -> 62.4 us  [local(): pl.pallas_call(functools.partial(kernel, scale), out_shape=(block, block,...]
    reshape x3 -> x0, local copies, waits for them, and re-layouts: 46.2 us -> none  [the longest x2 44.3 us: patches(): return jnp.concatenate(pieces, axis=-1).reshape(rows * cols, -1)]
    unnamed x14 -> x0, other arithmetic: 35.5 us -> none
    dot_general x5 -> x0, matrix products: 32.4 us -> none  [the longest x1 11.5 us: local(): jnp.dot(columns, kernel.reshape(-1, width), preferred_element_type=jnp.fl...]
    ppermute x10 -> x0, starting transfers between devices: 18.9 us -> none  [the longest x4 11.8 us: with_halo(): lax.ppermute(head, axis, [((i + 1) % count, i) for i in range(count)])]
    concatenate x4 -> x0, other arithmetic: 8.81 us -> none  [the longest x2 5.69 us: patches(): return jnp.concatenate(pieces, axis=-1).reshape(rows * cols, -1)]
  transfers between devices with their start and end apart: 11 -> 0, of which waited for: 4 -> 0; matrix products, arithmetic and copies ran while one was open for 13% -> 0% of each run, Pallas kernels for 0% -> 0%
where the time goes in v1:
time: 70.3 us; the launch traced here: 70.2 us
  Pallas kernels  62.4 us (89%)
  local copies, waits for them, and re-layouts  7.15 us (10%)
    pallas_call x1, Pallas kernels, local(): pl.pallas_call(functools.partial(kernel, scale), out_shape=(block, block,...  62.4 us
    unnamed x7, local copies, waits for them, and re-layouts  7.15 us

profile of v1, /device:TPU:1, one launch (start us, length us, event | category | flops | bytes accessed | tf_op | source)
XLA Modules:
  0.0 70.2 jit_solution(7312501232999831618)
XLA Ops:
  0.6 62.4 %shard_map.58 = (bf16[90,45,256]{2,1,0:T(8,128)(2,1)}, bf16[90,45,256]{2,1,0:T(8,128)(2,1)}, f32[9,4,4,16,256]{4,3,2,1,0:T(8,128)}) custom-call(bf16[90,45,256]{2,1,0:T(8,128)(2,1)} %x_hbm.1, bf16[3,3,256,256]{3,2,1,0:T(8,128)(2,1)} %w_hbm.1, bf16[90,45,256]{2,1,0:T(8,128)(2,1)} %c_hbm.1), custom_call_target="tpu_custom_call" | custom-call | flops 15000000512 | bytes 12000000 | tf_op jit(solution)/shard_map/pallas_call | solution.py:388
  63.0 0.0 copy-start.1
  63.1 3.3 %copy.9 = bf16[90,45,256]{2,1,0:T(8,128)(2,1)} copy(bf16[90,45,256]{2,1,0:T(8,128)(2,1)} %get-tuple-element.12) | data formatting | bytes 4147200
  66.3 0.0 copy-done.1
  66.3 0.0 copy-start
  66.3 1.4 %copy.10 = bf16[90,45,256]{2,1,0:T(8,128)(2,1)} copy(bf16[90,45,256]{2,1,0:T(8,128)(2,1)S(1)} %copy-done.1) | data formatting | bytes 4147200
  67.7 1.1 %copy-done = f32[9,4,4,16,256]{4,3,2,1,0:T(8,128)S(1)} copy-done((f32[9,4,4,16,256]{4,3,2,1,0:T(8,128)S(1)}, f32[9,4,4,16,256]{4,3,2,1,0:T(8,128)}, u32[]{:S(2)}) %copy-start) | copy-done | bytes 2359320
  68.8 1.4 %copy.11 = f32[3,3,256,256]{3,2,1,0:T(8,128)} copy(f32[3,3,256,256]{3,2,1,0:T(8,128)S(1)} %bitcast.1) | data formatting | bytes 4718592
Async XLA Ops:
  63.0 3.3 %copy-start.1 = (bf16[90,45,256]{2,1,0:T(8,128)(2,1)S(1)}, bf16[90,45,256]{2,1,0:T(8,128)(2,1)}, u32[]{:S(2)}) copy-start(bf16[90,45,256]{2,1,0:T(8,128)(2,1)} %get-tuple-element.13) | copy-start | bytes 6220804
  66.3 2.5 %copy-start = (f32[9,4,4,16,256]{4,3,2,1,0:T(8,128)S(1)}, f32[9,4,4,16,256]{4,3,2,1,0:T(8,128)}, u32[]{:S(2)}) copy-start(f32[9,4,4,16,256]{4,3,2,1,0:T(8,128)} %get-tuple-element.8) | copy-start | bytes 7077892

commit v2 on v1

v2 whole, which is shorter than its diff:
```python
import functools
import math

import jax
import jax.numpy as jnp
from jax import lax
from jax.experimental import pallas as pl
from jax.experimental.pallas import tpu as pltpu
from jax.sharding import PartitionSpec as P

MESH = pl.DeviceIdType.MESH
F32 = jnp.float32
BF16 = jnp.bfloat16

ROWS, COLS, CH = 90, 45, 256
PITCH = 48
FLAT = (ROWS + 2) * PITCH + 32
DEPTH = 4352
NX, NY, NZ = 4, 4, 8
TILE = 10
TILES = ROWS // TILE
TAPS = 9
WAITS = (2, 7, 12, 17, 19)
STEPS = TAPS + 2 * TILES


def rows_at(row, count):
    return pl.ds(pl.multiple_of(row * PITCH, 16), count)


def kernel(
    scale,
    x_hbm, w_hbm, c_hbm,
    out_v, grad_v, kg_v,
    x_in, c_in, w,
    xs, cs, xt, x_rows, c_rows, c_halo,
    col_send, col_recv, corner_send, corner_recv,
    term, pair_recv, half, plane_recv, line, final,
    load_sem,
    row_send_sem, row_recv_sem, col_send_sem, col_recv_sem, corner_send_sem, corner_recv_sem,
    ar_send_sem, ar_recv_sem,
):
    lat, lon = lax.axis_index("lat"), lax.axis_index("lon")
    x_hi, y = lat // 4, lat % 4
    x_lo, z, core = lon // 16, (lon // 2) % 8, lon % 2
    xc = x_hi * 2 + x_lo

    def device(xx, yy, zz, cc):
        return ((xx // 2) * 4 + yy, ((xx % 2) * 8 + zz) * 2 + cc)

    north, south = lat == 0, lat == 7
    across = (lon + 16) % 32
    up = (jnp.where(north, 0, lat - 1), jnp.where(north, across, lon))
    down = (jnp.where(south, 7, lat + 1), jnp.where(south, across, lon))
    left, right = (lat, (lon + 31) % 32), (lat, (lon + 1) % 32)
    other = device(xc, y, z, 1 - core)

    def plane_peer(d):
        return device((xc + d // 4) % NX, (y + d % 4) % NY, z, core)

    loads = [
        pltpu.make_async_copy(c_hbm, c_in, load_sem.at[0]),
        pltpu.make_async_copy(x_hbm, x_in, load_sem.at[1]),
        pltpu.make_async_copy(w_hbm, w, load_sem.at[2]),
    ]
    for load in loads:
        load.start()

    barrier = pltpu.get_barrier_semaphore()
    friends = [device(xc, y, (z + d) % NZ, core) for d in (4, 3, 5, 2, 6, 1, 7)]
    friends += [plane_peer(d) for d in range(1, 16)]
    friends += [up, down, left, right, other]
    for friend in friends:
        pl.semaphore_signal(barrier, inc=1, device_id=friend, device_id_type=MESH)
    pl.semaphore_wait(barrier, len(friends))

    def row_copies(which, source, target):
        to_up, to_down = jnp.where(north, 0, 1), jnp.where(south, 1, 0)
        return [
            pltpu.make_async_remote_copy(
                src_ref=source.at[0], dst_ref=target.at[to_up],
                send_sem=row_send_sem.at[which, 0], recv_sem=row_recv_sem.at[which, to_up],
                device_id=up, device_id_type=MESH,
            ),
            pltpu.make_async_remote_copy(
                src_ref=source.at[ROWS - 1], dst_ref=target.at[to_down],
                send_sem=row_send_sem.at[which, 1], recv_sem=row_recv_sem.at[which, to_down],
                device_id=down, device_id_type=MESH,
            ),
        ]

    def row_wait(which, target):
        for side in range(2):
            pltpu.make_async_copy(target.at[side], target.at[side], row_recv_sem.at[which, side]).wait()

    def col_copies(which):
        return [
            pltpu.make_async_remote_copy(
                src_ref=col_send.at[which, side], dst_ref=col_recv.at[which, side],
                send_sem=col_send_sem.at[which, side], recv_sem=col_recv_sem.at[which, side],
                device_id=to, device_id_type=MESH,
            )
            for side, to in ((0, right), (1, left))
        ]

    def corner_copies(which):
        return [
            pltpu.make_async_remote_copy(
                src_ref=corner_send.at[which, side], dst_ref=corner_recv.at[which, side],
                send_sem=corner_send_sem.at[which, side], recv_sem=corner_recv_sem.at[which, side],
                device_id=to, device_id_type=MESH,
            )
            for side, to in ((0, right), (1, left))
        ]

    def send_columns(which, block):
        for side, col in ((0, COLS - 1), (1, 0)):
            col_send[which, side] = block[:, col : col + 1, :].astype(F32)
            col_copies(which)[side].start()

    def send_corners(which, rows):
        for side, col in ((0, COLS - 1), (1, 0)):
            corner_send[which, side] = rows[:, col : col + 1, :].astype(F32)
            corner_copies(which)[side].start()

    def wait_corners(which):
        for side in range(2):
            pltpu.make_async_copy(
                corner_recv.at[which, side], corner_recv.at[which, side], corner_recv_sem.at[which, side]
            ).wait()

    def centred(row):
        return jnp.concatenate([row, jnp.zeros((PITCH - COLS, CH), BF16)], 0)

    def sideways(row, before, after):
        wide = row.astype(F32)
        pad = jnp.zeros((PITCH - COLS, CH), F32)
        return (
            (0, jnp.concatenate([before, wide, pad[1:]], 0).astype(BF16)),
            (2, jnp.concatenate([wide[1:], after, pad], 0).astype(BF16)),
        )

    def spread_centre(block, target):
        @pl.loop(0, ROWS, unroll=5)
        def _(r):
            target[1, rows_at(r + 1, PITCH), :] = centred(block[r])

        for b in range(3):
            target[b, 0:PITCH, :] = jnp.zeros((PITCH, CH), BF16)
            target[b, (ROWS + 1) * PITCH :, :] = jnp.zeros((FLAT - (ROWS + 1) * PITCH, CH), BF16)

    def spread_sides(which, block, target):
        for side in range(2):
            pltpu.make_async_copy(
                col_recv.at[which, side], col_recv.at[which, side], col_recv_sem.at[which, side]
            ).wait()

        @pl.loop(0, ROWS, unroll=5)
        def _(r):
            for b, value in sideways(block[r], col_recv[which, 0, r], col_recv[which, 1, r]):
                target[b, rows_at(r + 1, PITCH), :] = value

    def send_rows(which, block, rows):
        for copy in row_copies(which, block, rows):
            copy.start()

    loads[0].wait()
    send_rows(0, c_in, c_rows)
    send_columns(0, c_in)
    spread_centre(c_in, cs)
    loads[1].wait()
    spread_centre(x_in, xs)
    for i in range(DEPTH // 256):
        xt[:, i * 256 : (i + 1) * 256] = xs[1, PITCH + i * 256 : PITCH + (i + 1) * 256, :].T
    row_wait(0, c_rows)
    send_corners(0, c_rows)
    for end in range(2):
        c_halo[1, end] = centred(c_rows[end])
    send_rows(1, x_in, x_rows)
    send_columns(1, x_in)

    def tap_of(t):
        late = t - 5
        a_early = jnp.where(t == 1, 0, jnp.where(t == 2, 2, 1))
        b_early = jnp.where(t == 3, 0, jnp.where(t == 4, 2, 1))
        corner = t >= 5
        return (
            jnp.where(corner, (late // 2) * 2, a_early),
            jnp.where(corner, (late % 2) * 2, b_early),
        )

    top_tap = jnp.where(north, 0, 2)
    bottom_tap = jnp.where(south, 2, 0)

    def pair_copy(t):
        return pltpu.make_async_remote_copy(
            src_ref=term.at[t, 1 - core], dst_ref=pair_recv.at[t],
            send_sem=ar_send_sem.at[0, t], recv_sem=ar_recv_sem.at[0, t],
            device_id=other, device_id_type=MESH,
        )

    def remote(src, dst, phase, t, to):
        pltpu.make_async_remote_copy(
            src_ref=src, dst_ref=dst, send_sem=ar_send_sem.at[phase, t], recv_sem=ar_recv_sem.at[phase, t],
            device_id=to, device_id_type=MESH,
        ).start()

    def arrived(ref, phase, t):
        pltpu.make_async_copy(ref, ref, ar_recv_sem.at[phase, t]).wait()

    def to_plane(t):
        arrived(pair_recv.at[t], 0, t)
        half[t] = term[t, core] + pair_recv[t]
        for d in range(1, 16):
            piece = half.at[t, (xc + d // 4) % NX, (y + d % 4) % NY]
            remote(piece, plane_recv.at[t, d - 1], 1, t, plane_peer(d))

    def to_line(t):
        arrived(plane_recv.at[t], 1, t)
        parts = [half[t, xc, y]] + [plane_recv[t, d] for d in range(15)]
        while len(parts) > 1:
            parts = [parts[i] + parts[i + 1] for i in range(0, len(parts), 2)]
        line[t, z] = parts[0]
        for d in (4, 3, 5, 2, 6, 1, 7):
            remote(line.at[t, z], line.at[t, z], 2, t, device(xc, y, (z + d) % NZ, core))

    def from_line(t):
        arrived(line.at[t, 0:7], 2, t)
        parts = [line[t, i] for i in range(NZ)]
        while len(parts) > 1:
            parts = [parts[i] + parts[i + 1] for i in range(0, len(parts), 2)]
        final[t, core, xc, y] = parts[0] * scale
        piece = final.at[t, core, xc, y]
        for d in range(1, 16):
            remote(piece, piece, 3, t, plane_peer(d))

    def to_pair(t):
        arrived(plane_recv.at[t], 3, t)
        remote(final.at[t, core], final.at[t, core], 4, t, other)

    def finish(t):
        arrived(pair_recv.at[t], 4, t)
        a, b = tap_of(t)
        kg_v[a * 3 + b, :, :, :, :128] = final[t, 0]
        kg_v[a * 3 + b, :, :, :, 128:] = final[t, 1]

    plan = list(zip(WAITS, (to_plane, to_line, from_line, to_pair, finish)))

    def communicate(s, begin, end):
        for wait, phase in reversed(plan):
            if wait < end and TAPS + wait > begin:
                t = s - wait

                @pl.when((t >= 0) & (t < TAPS))
                def _():
                    phase(t)

    def weight_tap(t):
        a, b = tap_of(t)
        res = jnp.dot(xt[...], cs[2 - b, rows_at(2 - a, DEPTH), :], preferred_element_type=F32)
        term[t, 0] = res[:, :128].reshape(4, 4, 16, 128)
        term[t, 1] = res[:, 128:].reshape(4, 4, 16, 128)
        for side, tap, row in ((0, top_tap, 1), (1, bottom_tap, ROWS)):
            @pl.when(a == tap)
            def _():
                more = lax.dot_general(
                    xs[1, row * PITCH : row * PITCH + PITCH, :], c_halo[2 - b, side],
                    (((0,), (0,)), ((), ())), preferred_element_type=F32,
                )
                term[t, 0] += more[:, :128].reshape(4, 4, 16, 128)
                term[t, 1] += more[:, 128:].reshape(4, 4, 16, 128)
        pair_copy(t).start()

    def out_tile(i):
        acc = None
        for a in range(3):
            for b in range(3):
                part = jnp.dot(
                    xs[b, rows_at(i * TILE + a, TILE * PITCH), :], w[a, b], preferred_element_type=F32
                )
                acc = part if acc is None else acc + part
        out_v[pl.ds(i * TILE, TILE)] = acc.astype(BF16).reshape(TILE, PITCH, CH)[:, :COLS]

    def times_transposed(rows, weights):
        return lax.dot_general(rows, weights, (((1,), (1,)), ((), ())), preferred_element_type=F32)

    def grad_rows(row, count):
        acc = None
        for a in range(3):
            for b in range(3):
                part = times_transposed(cs[2 - b, rows_at(row + 2 - a, count * PITCH), :], w[a, b])
                acc = part if acc is None else acc + part
        return acc

    def grad_tile(i):
        grad_v[pl.ds(i * TILE, TILE)] = (
            grad_rows(i * TILE, TILE).astype(BF16).reshape(TILE, PITCH, CH)[:, :COLS]
        )
        for side, tile, row, tap in ((0, 0, 0, top_tap), (1, TILES - 1, ROWS - 1, bottom_tap)):
            @pl.when(i == tile)
            def _():
                acc = grad_rows(row, 1)
                for b in range(3):
                    acc = acc + times_transposed(c_halo[2 - b, side], w[tap, b])
                grad_v[row] = acc.astype(BF16)[:COLS]

    def edge_rows(which, rows):
        for end in range(2):
            for b, value in sideways(rows[end], corner_recv[which, 0, end], corner_recv[which, 1, end]):
                yield end, b, value

    @pl.loop(0, TAPS)
    def _(s):
        communicate(s, 0, TAPS)

        @pl.when(s == 2)
        def _():
            row_wait(1, x_rows)
            send_corners(1, x_rows)
            for end in range(2):
                place = slice(end * (ROWS + 1) * PITCH, end * (ROWS + 1) * PITCH + PITCH)
                xs[1, place, :] = centred(x_rows[end])

        @pl.when(s == 3)
        def _():
            spread_sides(0, c_in, cs)

        @pl.when(s == 5)
        def _():
            wait_corners(0)
            for end, b, value in edge_rows(0, c_rows):
                c_halo[b, end] = value

        weight_tap(s)

    loads[2].wait()
    spread_sides(1, x_in, xs)
    wait_corners(1)
    for end, b, value in edge_rows(1, x_rows):
        xs[b, end * (ROWS + 1) * PITCH : end * (ROWS + 1) * PITCH + PITCH, :] = value

    @pl.loop(TAPS, TAPS + TILES)
    def _(s):
        communicate(s, TAPS, TAPS + TILES)
        out_tile(s - TAPS)

    @pl.loop(TAPS + TILES, STEPS)
    def _(s):
        communicate(s, TAPS + TILES, STEPS)
        grad_tile(s - TAPS - TILES)

    last = TAPS + WAITS[-1]

    @pl.loop(STEPS, last)
    def _(s):
        communicate(s, STEPS, last)

    for which, block, rows in ((0, c_in, c_rows), (1, x_in, x_rows)):
        for copy in row_copies(which, block, rows) + col_copies(which) + corner_copies(which):
            copy.wait_send()

    def sent(ref, phase, t):
        pltpu.make_async_copy(ref, ref, ar_send_sem.at[phase, t]).wait()

    @pl.loop(0, TAPS)
    def _(t):
        for phase, ref in enumerate(
            (pair_recv.at[t], plane_recv.at[t], line.at[t, 0:7], plane_recv.at[t], pair_recv.at[t])
        ):
            sent(ref, phase, t)


def store_kernel(*refs):
    sems = refs[6]
    copies = [pltpu.make_async_copy(refs[i], refs[i + 3], sems.at[i]) for i in range(3)]
    for copy in copies:
        copy.start()
    for copy in copies:
        copy.wait()


def local(inputs, weights, cotangent):
    scale = 1.0 / math.sqrt(ROWS * COLS * lax.axis_size("lat") * lax.axis_size("lon"))
    block = pltpu.VMEM((ROWS, COLS, CH), BF16)
    anywhere = pl.BlockSpec(memory_space=pl.ANY)
    dma = pltpu.SemaphoreType.DMA
    outputs, grad, kg = pl.pallas_call(
        functools.partial(kernel, scale),
        out_shape=(block, block, pltpu.VMEM((TAPS, 4, 4, 16, CH), F32)),
        in_specs=[anywhere] * 3,
        out_specs=(pl.BlockSpec(memory_space=pltpu.VMEM),) * 3,
        scratch_shapes=[
            pltpu.VMEM((ROWS, COLS, CH), BF16),
            pltpu.VMEM((ROWS, COLS, CH), BF16),
            pltpu.VMEM((3, 3, CH, CH), BF16),
            pltpu.VMEM((3, FLAT, CH), BF16),
            pltpu.VMEM((3, FLAT, CH), BF16),
            pltpu.VMEM((CH, DEPTH), BF16),
            pltpu.VMEM((2, COLS, CH), BF16),
            pltpu.VMEM((2, COLS, CH), BF16),
            pltpu.VMEM((3, 2, PITCH, CH), BF16),
            pltpu.VMEM((2, 2, ROWS, 1, CH), F32),
            pltpu.VMEM((2, 2, ROWS, 1, CH), F32),
            pltpu.VMEM((2, 2, 2, 1, CH), F32),
            pltpu.VMEM((2, 2, 2, 1, CH), F32),
            pltpu.VMEM((TAPS, 2, 4, 4, 16, 128), F32),
            pltpu.VMEM((TAPS, 4, 4, 16, 128), F32),
            pltpu.VMEM((TAPS, 4, 4, 16, 128), F32),
            pltpu.VMEM((TAPS, 15, 16, 128), F32),
            pltpu.VMEM((TAPS, NZ, 16, 128), F32),
            pltpu.VMEM((TAPS, 2, 4, 4, 16, 128), F32),
            dma((3,)),
            dma((2, 2)),
            dma((2, 2)),
            dma((2, 2)),
            dma((2, 2)),
            dma((2, 2)),
            dma((2, 2)),
            dma((5, TAPS)),
            dma((5, TAPS)),
        ],
        compiler_params=pltpu.CompilerParams(
            collective_id=0, has_side_effects=True, vmem_limit_bytes=56 * 2**20
        ),
        cost_estimate=pl.CostEstimate(flops=15 * 10**9, bytes_accessed=12 * 10**6, transcendentals=0),
    )(inputs, weights, cotangent)
    outputs, grad, kg = pl.pallas_call(
        store_kernel,
        out_shape=tuple(jax.ShapeDtypeStruct(v.shape, v.dtype) for v in (outputs, grad, kg)),
        in_specs=[anywhere] * 3,
        out_specs=(anywhere,) * 3,
        scratch_shapes=[dma((3,))],
        compiler_params=pltpu.CompilerParams(vmem_limit_bytes=2**20),
    )(outputs, grad, kg)
    return outputs, grad, kg.reshape(3, 3, CH, CH)


def solution(mesh):
    in_specs = (P("lat", "lon", None), P(), P("lat", "lon", None))
    out_specs = (P("lat", "lon", None), P("lat", "lon", None), P())
    return jax.shard_map(local, mesh=mesh, in_specs=in_specs, out_specs=out_specs, check_vma=False)
```

time: 70.3 us -> 55.5 us (0.79)
  Pallas kernels: 62.4 us -> 54.8 us
  local copies, waits for them, and re-layouts: 7.15 us -> 0 us
    pallas_call x1, Pallas kernels: 62.4 us -> 51.9 us  [local(): pl.pallas_call(functools.partial(kernel, scale), out_shape=(block, block,...]
    unnamed x7 -> x0, local copies, waits for them, and re-layouts: 7.15 us -> none
    pallas_call x0 -> x1, Pallas kernels: none -> 2.89 us  [local(): pl.pallas_call(store_kernel, out_shape=tuple((jax.ShapeDtypeStruct(v.shap...]
where the time goes in v2:
time: 55.5 us
  Pallas kernels  54.8 us (99%)
  between operations  0.64 us (1%)
    pallas_call x1, Pallas kernels, local(): pl.pallas_call(functools.partial(kernel, scale), out_shape=(block, block,...  51.9 us
    pallas_call x1, Pallas kernels, local(): pl.pallas_call(store_kernel, out_shape=tuple((jax.ShapeDtypeStruct(v.shap...  2.89 us

profile of v2, /device:TPU:1, one launch (start us, length us, event | category | flops | bytes accessed | tf_op | source)
XLA Modules:
  0.0 55.5 jit_solution(13984804963232349409)
XLA Ops:
  0.6 51.9 %shard_map.58 = (bf16[90,45,256]{2,1,0:T(8,128)(2,1)S(1)}, bf16[90,45,256]{2,1,0:T(8,128)(2,1)S(1)}, f32[9,4,4,16,256]{4,3,2,1,0:T(8,128)S(1)}) custom-call(bf16[90,45,256]{2,1,0:T(8,128)(2,1)} %x_hbm.1, bf16[3,3,256,256]{3,2,1,0:T(8,128)(2,1)} %w_hbm.1, bf16[90,45,256]{2,1,0:T(8,128)(2,1)} %c_hbm.1), custom_call_target="tpu_custom_call" | custom-call | flops 15000000512 | bytes 12000000 | tf_op jit(solution)/shard_map/pallas_call | solution.py:387
  52.6 2.9 %shard_map.59 = (bf16[90,45,256]{2,1,0:T(8,128)(2,1)}, bf16[90,45,256]{2,1,0:T(8,128)(2,1)}, f32[9,4,4,16,256]{4,3,2,1,0:T(8,128)}) custom-call(bf16[90,45,256]{2,1,0:T(8,128)(2,1)S(1)} %get-tuple-element.9.refs_0_, bf16[90,45,256]{2,1,0:T(8,128)(2,1)S(1)} %get-tuple-element.10.refs_1_, f32[9,4,4,16,256]{4,3,2,1,0:T(8,128)S(1)} %get-tuple-element.11.refs_2_), custom_call_target="tpu_custom_call" | custom-call | tf_op jit(solution)/shard_map/pallas_call | solution.py:427

commit v3 on v2

--- a/solution.py
+++ b/solution.py
@@ -17,10 +17,11 @@
 FLAT = (ROWS + 2) * PITCH + 32
 DEPTH = 4352
 NX, NY, NZ = 4, 4, 8
-TILE = 10
+TILE = 15
 TILES = ROWS // TILE
 TAPS = 9
-WAITS = (2, 7, 12, 17, 19)
+WAITS = (2, 7, 11, 15, 17)
+PLANE_ORDER = (10, 5, 15, 7, 13, 2, 8, 6, 9, 14, 11, 1, 4, 3, 12)
 STEPS = TAPS + 2 * TILES
 
 
@@ -172,12 +173,6 @@
     spread_centre(x_in, xs)
     for i in range(DEPTH // 256):
         xt[:, i * 256 : (i + 1) * 256] = xs[1, PITCH + i * 256 : PITCH + (i + 1) * 256, :].T
-    row_wait(0, c_rows)
-    send_corners(0, c_rows)
-    for end in range(2):
-        c_halo[1, end] = centred(c_rows[end])
-    send_rows(1, x_in, x_rows)
-    send_columns(1, x_in)
 
     def tap_of(t):
         late = t - 5
@@ -211,7 +206,7 @@
     def to_plane(t):
         arrived(pair_recv.at[t], 0, t)
         half[t] = term[t, core] + pair_recv[t]
-        for d in range(1, 16):
+        for d in PLANE_ORDER:
             piece = half.at[t, (xc + d // 4) % NX, (y + d % 4) % NY]
             remote(piece, plane_recv.at[t, d - 1], 1, t, plane_peer(d))
 
@@ -231,7 +226,7 @@
             parts = [parts[i] + parts[i + 1] for i in range(0, len(parts), 2)]
         final[t, core, xc, y] = parts[0] * scale
         piece = final.at[t, core, xc, y]
-        for d in range(1, 16):
+        for d in PLANE_ORDER:
             remote(piece, piece, 3, t, plane_peer(d))
 
     def to_pair(t):
@@ -313,7 +308,19 @@
     def _(s):
         communicate(s, 0, TAPS)
 
+        @pl.when(s == 1)
+        def _():
+            row_wait(0, c_rows)
+            send_corners(0, c_rows)
+            for end in range(2):
+                c_halo[1, end] = centred(c_rows[end])
+            send_rows(1, x_in, x_rows)
+
         @pl.when(s == 2)
+        def _():
+            send_columns(1, x_in)
+
+        @pl.when(s == 6)
         def _():
             row_wait(1, x_rows)
             send_corners(1, x_rows)

time: 55.5 us -> 51.8 us (0.933)
  Pallas kernels: 54.8 us -> 51.1 us
    pallas_call x1, Pallas kernels: 51.9 us -> 48.2 us  [local(): pl.pallas_call(functools.partial(kernel, scale), out_shape=(block, block,...]
where the time goes in v3:
time: 51.8 us; the launch traced here: 51.7 us
  Pallas kernels  51.1 us (99%)
  between operations  0.64 us (1%)
    pallas_call x1, Pallas kernels, local(): pl.pallas_call(functools.partial(kernel, scale), out_shape=(block, block,...  48.2 us
    pallas_call x1, Pallas kernels, local(): pl.pallas_call(store_kernel, out_shape=tuple((jax.ShapeDtypeStruct(v.shap...  2.89 us

profile of v3, /device:TPU:1, one launch (start us, length us, event | category | flops | bytes accessed | tf_op | source)
XLA Modules:
  0.0 51.7 jit_solution(8604109853604426680)
XLA Ops:
  0.6 48.2 %shard_map.58 = (bf16[90,45,256]{2,1,0:T(8,128)(2,1)S(1)}, bf16[90,45,256]{2,1,0:T(8,128)(2,1)S(1)}, f32[9,4,4,16,256]{4,3,2,1,0:T(8,128)S(1)}) custom-call(bf16[90,45,256]{2,1,0:T(8,128)(2,1)} %x_hbm.1, bf16[3,3,256,256]{3,2,1,0:T(8,128)(2,1)} %w_hbm.1, bf16[90,45,256]{2,1,0:T(8,128)(2,1)} %c_hbm.1), custom_call_target="tpu_custom_call" | custom-call | flops 15000000512 | bytes 12000000 | tf_op jit(solution)/shard_map/pallas_call | solution.py:394
  48.8 2.9 %shard_map.59 = (bf16[90,45,256]{2,1,0:T(8,128)(2,1)}, bf16[90,45,256]{2,1,0:T(8,128)(2,1)}, f32[9,4,4,16,256]{4,3,2,1,0:T(8,128)}) custom-call(bf16[90,45,256]{2,1,0:T(8,128)(2,1)S(1)} %get-tuple-element.9.refs_0_, bf16[90,45,256]{2,1,0:T(8,128)(2,1)S(1)} %get-tuple-element.10.refs_1_, f32[9,4,4,16,256]{4,3,2,1,0:T(8,128)S(1)} %get-tuple-element.11.refs_2_), custom_call_target="tpu_custom_call" | custom-call | tf_op jit(solution)/shard_map/pallas_call | solution.py:434

commit v4 on v3

--- a/solution.py
+++ b/solution.py
@@ -356,25 +356,28 @@
         communicate(s, TAPS + TILES, STEPS)
         grad_tile(s - TAPS - TILES)
 
+    for which, block, rows in ((0, c_in, c_rows), (1, x_in, x_rows)):
+        for copy in row_copies(which, block, rows) + col_copies(which) + corner_copies(which):
+            copy.wait_send()
+
+    def sent(ref, phase, t):
+        pltpu.make_async_copy(ref, ref, ar_send_sem.at[phase, t]).wait()
+
+    @pl.loop(0, TAPS)
+    def _(t):
+        for phase, ref in enumerate((pair_recv.at[t], plane_recv.at[t], line.at[t, 0:7])):
+            sent(ref, phase, t)
+
     last = TAPS + WAITS[-1]
 
     @pl.loop(STEPS, last)
     def _(s):
         communicate(s, STEPS, last)
 
-    for which, block, rows in ((0, c_in, c_rows), (1, x_in, x_rows)):
-        for copy in row_copies(which, block, rows) + col_copies(which) + corner_copies(which):
-            copy.wait_send()
-
-    def sent(ref, phase, t):
-        pltpu.make_async_copy(ref, ref, ar_send_sem.at[phase, t]).wait()
-
     @pl.loop(0, TAPS)
     def _(t):
-        for phase, ref in enumerate(
-            (pair_recv.at[t], plane_recv.at[t], line.at[t, 0:7], plane_recv.at[t], pair_recv.at[t])
-        ):
-            sent(ref, phase, t)
+        sent(plane_recv.at[t], 3, t)
+        sent(pair_recv.at[t], 4, t)
 
 
 def store_kernel(*refs):

time: 51.8 us -> 51.7 us (level)
  no operation moved by 1% of the time
where the time goes in v4:
time: 51.7 us
  Pallas kernels  51 us (99%)
  between operations  0.64 us (1%)
    pallas_call x1, Pallas kernels, local(): pl.pallas_call(functools.partial(kernel, scale), out_shape=(block, block,...  48.1 us
    pallas_call x1, Pallas kernels, local(): pl.pallas_call(store_kernel, out_shape=tuple((jax.ShapeDtypeStruct(v.shap...  2.89 us

profile of v4, /device:TPU:1, one launch (start us, length us, event | category | flops | bytes accessed | tf_op | source)
XLA Modules:
  0.0 51.7 jit_solution(14594304636694835069)
XLA Ops:
  0.6 48.1 %shard_map.58 = (bf16[90,45,256]{2,1,0:T(8,128)(2,1)S(1)}, bf16[90,45,256]{2,1,0:T(8,128)(2,1)S(1)}, f32[9,4,4,16,256]{4,3,2,1,0:T(8,128)S(1)}) custom-call(bf16[90,45,256]{2,1,0:T(8,128)(2,1)} %x_hbm.1, bf16[3,3,256,256]{3,2,1,0:T(8,128)(2,1)} %w_hbm.1, bf16[90,45,256]{2,1,0:T(8,128)(2,1)} %c_hbm.1), custom_call_target="tpu_custom_call" | custom-call | flops 15000000512 | bytes 12000000 | tf_op jit(solution)/shard_map/pallas_call | solution.py:397
  48.8 2.9 %shard_map.59 = (bf16[90,45,256]{2,1,0:T(8,128)(2,1)}, bf16[90,45,256]{2,1,0:T(8,128)(2,1)}, f32[9,4,4,16,256]{4,3,2,1,0:T(8,128)}) custom-call(bf16[90,45,256]{2,1,0:T(8,128)(2,1)S(1)} %get-tuple-element.9.refs_0_, bf16[90,45,256]{2,1,0:T(8,128)(2,1)S(1)} %get-tuple-element.10.refs_1_, f32[9,4,4,16,256]{4,3,2,1,0:T(8,128)S(1)} %get-tuple-element.11.refs_2_), custom_call_target="tpu_custom_call" | custom-call | tf_op jit(solution)/shard_map/pallas_call | solution.py:437
